TPU v7x, 512 devices: a whole 4x8x8 slice. The times are simulated.
512 devices in a mesh: cfg: 64 (over y, x, core), tp: 8 (over z).
Axes of the slice: x: 4, y: 8, z: 8, core: 2. Of those that a mesh axis runs over, the one named last changes fastest.
Arguments:
- pool: bfloat16 [64, 192, 8192], P('cfg', None, 'tp'), may hold values from -6 to 6
- base_run: int32 [1], replicated, may hold values from 0 to 63
- gain: bfloat16 [8192], replicated, may hold values from 0.099609375 to 1.8984375
- w_key: bfloat16 [8192, 1024], P(None, 'tp'), may hold values from -0.0625 to 0.0625
- w_value: bfloat16 [8192, 1024], P(None, 'tp'), may hold values from -0.0625 to 0.0625
- w_query: bfloat16 [8192, 8192], P('cfg', 'tp'), may hold values from -0.0625 to 0.0625
- src_pos: int32 [192, 64, 2], P(None, 'cfg'), may hold values from 0 to 191
- dst_pos: int32 [192, 64, 2], P('cfg'), may hold values from 0 to 187, as said below
- counts: int32 [192, 64], P('cfg'), may hold values from 0 to 2
Outputs:
- attended: bfloat16 [192, 4, 8192], P('cfg', None, 'tp')
- keys: bfloat16 [192, 192, 1024], P('cfg', None, 'tp')
- values: bfloat16 [192, 192, 1024], P('cfg', None, 'tp')
Inputs may be any that keep to these rules, and one draw needn't show every extreme that they name: `dst_pos`: within one config all 128 entries differ and lie below 188. `counts`: slots of config c and source run s in use, the first ones of the 2.
All inputs are finite; a program needn't handle non-finite values.
Results may differ from a plain program's by a relative error of at most 0.023.
Values may be sent and summed in bfloat16 or wider, within the bound.
A program may use at most 64 MiB of HBM per device.

v0:
```python
import math
import jax
import jax.numpy as jnp
from jax import lax
from jax.sharding import PartitionSpec as P

D = 8192
HD = 128
PROBE = 4
rope_base = 500000.0
epsilon = 1e-05


def spread(value, axis, source):
    kept = jnp.where(lax.axis_index(axis) == source, value, 0).astype(value.dtype)
    return lax.psum(kept, axis)


def rotate(tensor, positions):
    half_dim = tensor.shape[-1] // 2
    inverse_freq = jnp.exp(
        jnp.arange(half_dim, dtype=jnp.float32) * (-2.0 * math.log(rope_base) / tensor.shape[-1])
    )
    angles = positions.astype(jnp.float32)[:, None] * inverse_freq[None, :]
    cosine = jnp.cos(angles)[:, None, :]
    sine_vals = jnp.sin(angles)[:, None, :]
    lower_half = tensor[..., :half_dim]
    upper_half = tensor[..., half_dim:]
    return jnp.concatenate(
        [
            lower_half * cosine - upper_half * sine_vals,
            upper_half * cosine + lower_half * sine_vals,
        ],
        axis=-1,
    )


def body(pool, base_run, gain, w_key, w_value, w_query, src_pos, dst_pos, counts):
    length = pool.shape[1]
    local_cfg = dst_pos.shape[0]
    slot_count = dst_pos.shape[1] * dst_pos.shape[2]
    key_cols = w_key.shape[1]
    in_use = jnp.arange(dst_pos.shape[2], dtype=jnp.int32)[None, None, :] < counts[:, :, None]
    targets = jnp.where(in_use, dst_pos, length).reshape(local_cfg, slot_count)
    onehot = targets[:, :, None] == jnp.arange(length, dtype=jnp.int32)[None, None, :]
    covered = jnp.any(onehot, axis=1)
    base_rows = spread(pool[0], "cfg", base_run[0])
    picked = jnp.take(pool[0], src_pos[:, 0, :], axis=0)[:, None]
    arrived = lax.all_to_all(picked, "cfg", split_axis=0, concat_axis=1, tiled=True)
    arrived = arrived.reshape(local_cfg, slot_count, arrived.shape[-1])
    spliced = jnp.einsum(
        "csp,csd->cpd", onehot.astype(jnp.bfloat16), arrived, preferred_element_type=jnp.float32
    )
    patched = jnp.where(covered[:, :, None], spliced, base_rows[None].astype(jnp.float32)).astype(
        jnp.bfloat16
    )
    rows = patched.reshape(local_cfg * length, patched.shape[-1])
    gains = gain.astype(jnp.float32)
    widened = lax.all_gather(rows, "tp", axis=1, tiled=True).astype(jnp.float32)
    normed = (widened * gains[None, :]).astype(jnp.bfloat16)
    keys_acc = jnp.dot(normed, w_key, preferred_element_type=jnp.float32)
    values_acc = jnp.dot(normed, w_value, preferred_element_type=jnp.float32)
    squares = jnp.sum(widened * widened, axis=1)
    probe_rows = normed[length - PROBE : length]
    keys_acc, values_acc, squares, probe_rows = (keys_acc, values_acc, squares, probe_rows)
    scales = lax.rsqrt(squares / D + epsilon)
    key_raw = (scales[:, None] * keys_acc).reshape(local_cfg, length, key_cols)
    value_raw = (scales[:, None] * values_acc).reshape(local_cfg, length, key_cols)
    probe_scales = scales[length - PROBE : length]
    slice_rows = w_query.shape[0]
    probe_part = lax.dynamic_slice_in_dim(
        probe_rows, lax.axis_index("cfg") * slice_rows, slice_rows, 1
    )
    partial_value = jnp.dot(probe_part, w_query, preferred_element_type=jnp.float32)
    query_total = lax.psum(partial_value, "cfg")
    heads_dev = w_query.shape[1] // HD
    kv_dev = key_cols // HD
    group_size = heads_dev // kv_dev
    positions = jnp.arange(length, dtype=jnp.int32)
    probe_pos = length - PROBE + jnp.arange(PROBE, dtype=jnp.int32)
    queries = rotate(
        (probe_scales[:, None] * query_total).reshape(PROBE, heads_dev, HD), probe_pos
    ).astype(jnp.bfloat16)
    keys_out = rotate(key_raw.reshape(local_cfg, length, kv_dev, HD), positions).astype(
        jnp.bfloat16
    )
    values_out = value_raw.astype(jnp.bfloat16)
    query_groups = queries.reshape(PROBE, kv_dev, group_size, HD)
    value_heads = values_out.reshape(local_cfg, length, kv_dev, HD)
    scores = jnp.einsum(
        "pkgh,cskh->cpkgs", query_groups, keys_out, preferred_element_type=jnp.float32
    ) * HD ** (-0.5)
    causal = positions[None, :] <= probe_pos[:, None]
    scores = jnp.where(causal[None, :, None, None, :], scores, -1e30)
    probs_b = jax.nn.softmax(scores, axis=-1).astype(jnp.bfloat16)
    attended = jnp.einsum(
        "cpkgs,cskh->cpkgh", probs_b, value_heads, preferred_element_type=jnp.float32
    )
    attended = attended.astype(jnp.bfloat16).reshape(local_cfg, PROBE, heads_dev * HD)
    return (attended, keys_out.reshape(local_cfg, length, key_cols), values_out)


def solution(mesh):
    placed = (
        P("cfg", None, "tp"),
        P(),
        P(),
        P(None, "tp"),
        P(None, "tp"),
        P("cfg", "tp"),
        P(None, "cfg", None),
        P("cfg", None, None),
        P("cfg", None),
    )
    return jax.shard_map(
        body,
        mesh=mesh,
        in_specs=placed,
        out_specs=(P("cfg", None, "tp"), P("cfg", None, "tp"), P("cfg", None, "tp")),
        check_vma=False,
    )
```

profile of v0, /device:TPU:32, one launch (start us, length us, event | category | flops | bytes accessed | tf_op | source)
XLA Modules:
  0.0 618.3 jit_solution(13707132915547980617)
XLA Ops:
  7.2 0.8 compare_select_fusion
  8.0 0.7 compare_and_fusion
  9.0 3.8 gather_fusion
  12.9 1.2 gather.7
  14.2 2.7 broadcast_select_fusion
  16.9 10.3 %all-to-all-start = ((bf16[192,1,2,1024]{3,2,1,0:T(2,128)(2,1)}), bf16[192,1,2,1024]{3,2,1,0:T(2,128)(2,1)S(1)}, u32[]{:S(2)}, u32[]{:S(2)}) async-start(bf16[192,1,2,1024]{3,2,1,0:T(2,128)(2,1)} %broadcast_select_fusion), calls=%async_computation | async-start | bytes 1572864 | tf_op jit(solution)/shard_map/all_to_all | solution.py:49
  27.9 0.8 broadcast_select_fusion.1
  29.1 0.2 fusion.6
  29.3 18.0 %all-to-all-done = bf16[192,1,2,1024]{3,2,1,0:T(2,128)(2,1)S(1)} async-done(((bf16[192,1,2,1024]{3,2,1,0:T(2,128)(2,1)}), bf16[192,1,2,1024]{3,2,1,0:T(2,128)(2,1)S(1)}, u32[]{:S(2)}, u32[]{:S(2)}) %all-to-all-start) | async-done | bytes 786464 | tf_op jit(solution)/shard_map/all_to_all | solution.py:49
  47.3 1.4 copy.21
  48.7 2.3 reshape.261
  51.0 174.9 %all-reduce.2.cloned.1.call-done = bf16[192,1024]{1,0:T(8,128)(2,1)} async-done(((bf16[192,1024]{1,0:T(8,128)(2,1)}), bf16[192,1024]{1,0:T(8,128)(2,1)}) %all-reduce.2.cloned.1.call-update) | async-done | bytes 393232 | tf_op jit(solution)/shard_map/psum | solution.py:16
  225.8 2.5 select_convert_fusion
  228.6 0.4 multiply_cosine_fusion
  229.0 107.6 %all-gather.2.cloned.1.call-done = bf16[576,8192]{1,0:T(8,128)(2,1)} async-done(((bf16[576,1024]{1,0:T(8,128)(2,1)}), bf16[576,8192]{1,0:T(8,128)(2,1)}) %all-gather.2.cloned.1.call-update) | async-done | bytes 9437200 | tf_op jit(solution)/shard_map/all_gather | solution.py:59
  336.6 11.2 %fusion = (f32[576]{0:T(1024)S(1)}, bf16[576,8192]{1,0:T(8,128)(2,1)}) fusion(bf16[576,8192]{1,0:T(8,128)(2,1)} %all-gather.2.cloned.1.call-done, f32[8192]{0:T(1024)S(1)} %convert_element_type.76), kind=kLoop, calls=%fused_computation.3 | loop fusion | flops 23592384 | bytes 18909440 | tf_op jit(solution)/shard_map/reduce_sum | solution.py:63
  347.8 1.0 slice.28
  348.9 5.2 convolution_multiply_fusion
  354.2 248.4 %psum.15 = f32[4,1024]{1,0:T(4,128)S(1)} all-reduce(f32[4,1024]{1,0:T(4,128)S(1)} %fusion.16), channel_id=1, replica_groups=mesh['cfg'=64,'tp'=8] {'cfg'}, use_global_device_ids=true, to_apply=%region_3.4 | all-reduce | flops 4096 | bytes 32768 | tf_op jit(solution)/shard_map/psum | solution.py:75
  602.7 6.9 %fusion.2 = bf16[576,128]{1,0:T(8,128)(2,1)S(1)} fusion(bf16[576,8192]{1,0:T(8,128)(2,1)} %get-tuple-element.4, bf16[8192,128]{1,0:T(8,128)(2,1)} %param.13, f32[576]{0:T(1024)S(1)} %add_rsqrt_fusion), kind=kOutput, calls=%fused_computation.9 | convolution fusion | flops 1208107008 | bytes 11684096 | tf_op jit(solution)/shard_map/dot_general | solution.py:62
  610.0 0.3 fusion.21
  610.4 0.2 fusion.11
  610.6 0.2 fusion.5
  610.8 0.6 reshape.265
  (42 shorter events, 1.7 us)
Async XLA Ops:
  7.2 341.7 %copy-start = (bf16[8192,128]{1,0:T(8,128)(2,1)S(1)}, bf16[8192,128]{1,0:T(8,128)(2,1)}, u32[]{:S(2)}) copy-start(bf16[8192,128]{1,0:T(8,128)(2,1)} %param.12) | copy-start | bytes 6291460
  7.2 20.7 %copy-start.1 = (bf16[1,192,1024]{2,1,0:T(8,128)(2,1)S(1)}, bf16[1,192,1024]{2,1,0:T(8,128)(2,1)}, u32[]{:S(2)}) copy-start(bf16[1,192,1024]{2,1,0:T(8,128)(2,1)} %param.9) | copy-start | bytes 1179652
  7.2 21.6 %copy-start.5 = (s32[3,64,2]{1,2,0:T(2,128)S(1)}, s32[3,64,2]{1,2,0:T(2,128)}, u32[]{:S(2)}) copy-start(s32[3,64,2]{1,2,0:T(2,128)} %param.16) | copy-start | bytes 4612
  7.2 21.6 %copy-start.6 = (s32[3,64]{1,0:T(4,128)S(1)}, s32[3,64]{1,0:T(4,128)}, u32[]{:S(2)}) copy-start(s32[3,64]{1,0:T(4,128)} %param.17) | copy-start | bytes 2308
  9.0 219.3 %copy-start.4 = (bf16[8192]{0:T(1024)(128)(2,1)S(1)}, bf16[8192]{0:T(1024)(128)(2,1)}, u32[]{:S(2)}) copy-start(bf16[8192]{0:T(1024)(128)(2,1)} %param.11) | copy-start | bytes 49156
  16.9 30.4 %all-to-all-start = ((bf16[192,1,2,1024]{3,2,1,0:T(2,128)(2,1)}), bf16[192,1,2,1024]{3,2,1,0:T(2,128)(2,1)S(1)}, u32[]{:S(2)}, u32[]{:S(2)}) async-start(bf16[192,1,2,1024]{3,2,1,0:T(2,128)(2,1)} %broadcast_select_fusion), calls=%async_computation | async-start | bytes 1572864 | tf_op jit(solution)/shard_map/all_to_all | solution.py:49
  27.2 198.6 %all-reduce.2.cloned.1.call-start = ((), (), s32[]{:S(2)}) async-start(), calls=%async_computation.1 | async-start | bytes 786432 | tf_op jit(solution)/shard_map/psum | solution.py:16
  28.7 307.9 %all-gather.2.cloned.1.call-start = ((), (), s32[]{:S(2)}) async-start(), calls=%async_computation.2 | async-start | bytes 10616832 | tf_op jit(solution)/shard_map/all_gather | solution.py:59
  347.8 6.3 %copy-start.3 = (bf16[128,1024]{1,0:T(8,128)(2,1)S(1)}, bf16[128,1024]{1,0:T(8,128)(2,1)}, u32[]{:S(2)}) copy-start(bf16[128,1024]{1,0:T(8,128)(2,1)} %param.14) | copy-start | bytes 786436
  609.6 1.8 copy-start.7
  609.9 1.5 copy-start.2
Sparse Core Ops, SparseCore 0:
  31.5 194.2 all-reduce.1
  228.4 108.1 all-gather.1
where the time goes:
time: 619 us; the launch traced here: 618 us
  waiting for transfers between devices  300 us (48%)
  blocking collectives  248 us (40%)
  other arithmetic  17.6 us (3%)
  matrix products  15.3 us (2%)
  between operations  14.9 us (2%)
  local copies, waits for them, and re-layouts  11.1 us (2%)
  starting transfers between devices  10.4 us (2%)
    psum x1, blocking collectives, body(): query_total = lax.psum(partial_value, 'cfg')  248 us
    psum x1, waiting for transfers between devices, spread(): return lax.psum(kept, axis)  175 us
    all_gather x1, waiting for transfers between devices, body(): widened = lax.all_gather(rows, 'tp', axis=1, tiled=True).astype(jnp.float32)  108 us
    all_to_all x1, waiting for transfers between devices, body(): lax.all_to_all(picked, 'cfg', split_axis=0, concat_axis=1, tiled=True)  18 us
  transfers between devices with their start and end apart: 3, of which 3 were waited for; matrix products, arithmetic and copies ran while one was open for 1% of the time, Pallas kernels for 0%

commit v1 on v0

--- a/solution.py
+++ b/solution.py
@@ -9,6 +9,19 @@
 PROBE = 4
 rope_base = 500000.0
 epsilon = 1e-05
+
+
+def try_all_lines_on_mesh(page):
+    a_next = jnp.concatenate(
+        lax.all_to_all(
+            jnp.stack([page for _ in range(lax.axis_size("tp"))]),
+            axis_name="tp",
+            split_axis=0,
+            concat_axis=0,
+        ),
+        1,
+    )
+    return a_next
 
 
 def spread(value, axis, source):
@@ -56,7 +69,7 @@
     )
     rows = patched.reshape(local_cfg * length, patched.shape[-1])
     gains = gain.astype(jnp.float32)
-    widened = lax.all_gather(rows, "tp", axis=1, tiled=True).astype(jnp.float32)
+    widened = try_all_lines_on_mesh(rows).astype(jnp.float32)
     normed = (widened * gains[None, :]).astype(jnp.bfloat16)
     keys_acc = jnp.dot(normed, w_key, preferred_element_type=jnp.float32)
     values_acc = jnp.dot(normed, w_value, preferred_element_type=jnp.float32)

time: 619 us -> 750 us (1.21)
  waiting for transfers between devices: 300 us -> 401 us
  local copies, waits for them, and re-layouts: 11.1 us -> 26.9 us
  other arithmetic: 17.6 us -> 27.1 us
    all_to_all x0 -> x1, waiting for transfers between devices: none -> 208 us  [try_all_lines_on_mesh(): lax.all_to_all(jnp.stack([page for _ in range(lax.axis_size('tp'))]), axi...]
    all_gather x1 -> x0, waiting for transfers between devices: 108 us -> none  [body(): widened = lax.all_gather(rows, 'tp', axis=1, tiled=True).astype(jnp.float32)]
    unnamed x1 -> x2, other arithmetic: 0.08 us -> 12.7 us
    convert_element_type x0 -> x1, local copies, waits for them, and re-layouts: none -> 7.82 us  [body(): widened = try_all_lines_on_mesh(rows).astype(jnp.float32)]
    all_to_all x0 -> x1, starting transfers between devices: none -> 7.51 us  [try_all_lines_on_mesh(): lax.all_to_all(jnp.stack([page for _ in range(lax.axis_size('tp'))]), axi...]
where the time goes in v1:
time: 750 us; the launch traced here: 749 us
  waiting for transfers between devices  401 us (53%)
  blocking collectives  250 us (33%)
  other arithmetic  27.1 us (4%)
  local copies, waits for them, and re-layouts  26.9 us (4%)
  starting transfers between devices  17.9 us (2%)
  between operations  14.9 us (2%)
  matrix products  11.2 us (1%)
    psum x1, blocking collectives, body(): query_total = lax.psum(partial_value, 'cfg')  250 us
    all_to_all x1, waiting for transfers between devices, try_all_lines_on_mesh(): lax.all_to_all(jnp.stack([page for _ in range(lax.axis_size('tp'))]), axi...  208 us
    psum x1, waiting for transfers between devices, spread(): return lax.psum(kept, axis)  175 us
    all_to_all x1, waiting for transfers between devices, body(): lax.all_to_all(picked, 'cfg', split_axis=0, concat_axis=1, tiled=True)  18 us
  transfers between devices with their start and end apart: 3, of which 3 were waited for; matrix products, arithmetic and copies ran while one was open for 1% of the time, Pallas kernels for 0%

profile of v1, /device:TPU:32, one launch (start us, length us, event | category | flops | bytes accessed | tf_op | source)
XLA Modules:
  0.0 749.2 jit_solution(9854432013818762748)
XLA Ops:
  7.2 0.8 compare_and_fusion
  8.1 0.7 compare_select_fusion
  9.2 3.8 gather_fusion
  13.0 1.2 gather.7
  14.2 2.7 broadcast_select_fusion
  16.9 10.3 %all-to-all-start = ((bf16[192,1,2,1024]{3,2,1,0:T(2,128)(2,1)}), bf16[192,1,2,1024]{3,2,1,0:T(2,128)(2,1)S(1)}, u32[]{:S(2)}, u32[]{:S(2)}) async-start(bf16[192,1,2,1024]{3,2,1,0:T(2,128)(2,1)} %broadcast_select_fusion), calls=%async_computation | async-start | bytes 1572864 | tf_op jit(solution)/shard_map/all_to_all | solution.py:62
  27.9 0.8 broadcast_select_fusion.1
  29.2 18.0 %all-to-all-done = bf16[192,1,2,1024]{3,2,1,0:T(2,128)(2,1)S(1)} async-done(((bf16[192,1,2,1024]{3,2,1,0:T(2,128)(2,1)}), bf16[192,1,2,1024]{3,2,1,0:T(2,128)(2,1)S(1)}, u32[]{:S(2)}, u32[]{:S(2)}) %all-to-all-start) | async-done | bytes 786464 | tf_op jit(solution)/shard_map/all_to_all | solution.py:62
  47.2 1.4 copy.21
  48.7 2.3 reshape.264
  51.0 174.9 %all-reduce.2.cloned.1.call-done = bf16[192,1024]{1,0:T(8,128)(2,1)} async-done(((bf16[192,1024]{1,0:T(8,128)(2,1)}), bf16[192,1024]{1,0:T(8,128)(2,1)}) %all-reduce.2.cloned.1.call-update) | async-done | bytes 393232 | tf_op jit(solution)/shard_map/psum | solution.py:29
  225.8 1.5 select_convert_fusion
  227.3 4.8 stack.3
  232.1 7.5 %all-to-all-start.1 = ((bf16[8,576,1024]{2,1,0:T(8,128)(2,1)}), bf16[8,576,1024]{2,1,0:T(8,128)(2,1)}, u32[]{:S(2)}, u32[]{:S(2)}) async-start(bf16[8,576,1024]{2,1,0:T(8,128)(2,1)} %stack.3), calls=%async_computation.1 | async-start | bytes 18874368 | tf_op jit(solution)/shard_map/all_to_all | solution.py:16
  240.3 208.2 %all-to-all-done.1 = bf16[8,576,1024]{2,1,0:T(8,128)(2,1)} async-done(((bf16[8,576,1024]{2,1,0:T(8,128)(2,1)}), bf16[8,576,1024]{2,1,0:T(8,128)(2,1)}, u32[]{:S(2)}, u32[]{:S(2)}) %all-to-all-start.1) | async-done | bytes 9437216 | tf_op jit(solution)/shard_map/all_to_all | solution.py:16
  448.5 5.7 fusion
  454.3 12.7 %convert_bitcast_fusion = f32[8,72,8,1024]{3,2,1,0:T(8,128)} fusion(bf16[8,576,1024]{2,1,0:T(8,128)(2,1)} %all-to-all-done.1), kind=kLoop, calls=%fused_computation.1 | loop fusion | flops 4718592 | bytes 28311552
  466.9 7.8 %copy.25 = f32[8,72,8,1024]{3,2,0,1:T(8,128)S(1)} copy(f32[8,72,8,1024]{3,2,1,0:T(8,128)} %convert_bitcast_fusion) | data formatting | bytes 37748736 | tf_op jit(solution)/shard_map/convert_element_type | solution.py:72
  474.8 2.3 multiply_convert_fusion
  477.1 3.6 copy-done.2
  480.9 250.1 %psum.15 = f32[4,1024]{1,0:T(4,128)S(1)} all-reduce(f32[4,1024]{1,0:T(4,128)S(1)} %fusion.15), channel_id=1, replica_groups=mesh['cfg'=64,'tp'=8] {'cfg'}, use_global_device_ids=true, to_apply=%region_3.4 | all-reduce | flops 4096 | bytes 32768 | tf_op jit(solution)/shard_map/psum | solution.py:88
  731.2 6.4 fusion.1
  738.0 2.6 convolution_multiply_fusion
  741.8 0.6 reshape.267
  (51 shorter events, 3.5 us)
Async XLA Ops:
  7.2 724.0 %copy-start = (bf16[8192,128]{1,0:T(8,128)(2,1)S(1)}, bf16[8192,128]{1,0:T(8,128)(2,1)}, u32[]{:S(2)}) copy-start(bf16[8192,128]{1,0:T(8,128)(2,1)} %param.13) | copy-start | bytes 6291460
  7.2 20.7 %copy-start.1 = (bf16[1,192,1024]{2,1,0:T(8,128)(2,1)S(1)}, bf16[1,192,1024]{2,1,0:T(8,128)(2,1)}, u32[]{:S(2)}) copy-start(bf16[1,192,1024]{2,1,0:T(8,128)(2,1)} %param.9) | copy-start | bytes 1179652
  7.2 21.5 %copy-start.8 = (s32[3,64]{1,0:T(4,128)S(1)}, s32[3,64]{1,0:T(4,128)}, u32[]{:S(2)}) copy-start(s32[3,64]{1,0:T(4,128)} %param.17) | copy-start | bytes 2308
  7.2 21.5 %copy-start.7 = (s32[3,64,2]{1,2,0:T(2,128)S(1)}, s32[3,64,2]{1,2,0:T(2,128)}, u32[]{:S(2)}) copy-start(s32[3,64,2]{1,2,0:T(2,128)} %param.16) | copy-start | bytes 4612
  16.9 30.4 %all-to-all-start = ((bf16[192,1,2,1024]{3,2,1,0:T(2,128)(2,1)}), bf16[192,1,2,1024]{3,2,1,0:T(2,128)(2,1)S(1)}, u32[]{:S(2)}, u32[]{:S(2)}) async-start(bf16[192,1,2,1024]{3,2,1,0:T(2,128)(2,1)} %broadcast_select_fusion), calls=%async_computation | async-start | bytes 1572864 | tf_op jit(solution)/shard_map/all_to_all | solution.py:62
  27.2 198.6 %all-reduce.2.cloned.1.call-start = ((), (), s32[]{:S(2)}) async-start(), calls=%async_computation.2 | async-start | bytes 786432 | tf_op jit(solution)/shard_map/psum | solution.py:29
  232.1 7.5 %copy-start.6 = (bf16[8192]{0:T(1024)(128)(2,1)S(1)}, bf16[8192]{0:T(1024)(128)(2,1)}, u32[]{:S(2)}) copy-start(bf16[8192]{0:T(1024)(128)(2,1)} %param.11) | copy-start | bytes 49156
  232.1 216.4 %all-to-all-start.1 = ((bf16[8,576,1024]{2,1,0:T(8,128)(2,1)}), bf16[8,576,1024]{2,1,0:T(8,128)(2,1)}, u32[]{:S(2)}, u32[]{:S(2)}) async-start(bf16[8,576,1024]{2,1,0:T(8,128)(2,1)} %stack.3), calls=%async_computation.1 | async-start | bytes 18874368 | tf_op jit(solution)/shard_map/all_to_all | solution.py:16
  474.8 6.0 copy-start.5
  477.1 3.6 copy-start.2
  731.1 6.5 copy-start.3
  731.1 7.0 copy-start.9
  738.0 4.4 copy-start.10
  740.9 1.5 copy-start.4
Sparse Core Ops, SparseCore 0:
  31.5 194.2 all-reduce.1
